TPU v7x, 256 devices: a whole 4x4x8 slice. The times are simulated.
256 devices in a mesh: dp: 32 (over z, x), mp: 8 (over y, core).
Axes of the slice: x: 4, y: 4, z: 8, core: 2. Of those that a mesh axis runs over, the one named last changes fastest.
Arguments:
- tokens: bfloat16 [12288, 8192], P('dp', 'mp'), may hold values from -6 to 6
- frozen_base_weight: bfloat16 [8192, 8192], P('mp', 'dp'), may hold values from -0.0625 to 0.0625
- tenant_down_factors: bfloat16 [64, 8192, 64], P('dp', 'mp'), may hold values from -0.0625 to 0.0625
- tenant_up_factors: bfloat16 [64, 8192, 64], P('dp', 'mp'), may hold values from -0.75 to 0.75
- cotangent: bfloat16 [12288, 8192], P('dp', 'mp'), may hold values from -6 to 6
- block_tenant_index: int32 [96], replicated, may hold values from 0 to 63
- ranks: int32 [64], replicated, may hold values from 8 to 64
Outputs:
- layer_out: bfloat16 [12288, 8192], P('dp', 'mp')
- input_grad: bfloat16 [12288, 8192], P('dp', 'mp')
- down_grad: float32 [64, 8192, 64], P('dp', 'mp')
- up_grad: float32 [64, 8192, 64], P('dp', 'mp')
Inputs may be any that keep to these rules, and one draw needn't show every extreme that they name: `block_tenant_index`: tenant of each block of 128 consecutive rows; some tenants own many blocks, some none. `ranks`: rank columns at or past a tenant's rank are unused.
All inputs are finite; a program needn't handle non-finite values.
Results may differ from a plain program's by a relative error of at most 0.017.
Values may be sent and summed in bfloat16 or wider, within the bound.
A program may use at most 128 MiB of HBM per device.

v0:
```python
import jax
import jax.numpy as jnp
from jax import lax
from jax.sharding import PartitionSpec as P

BLOCK = 128


def local(
    tokens,
    frozen_base_weight,
    tenant_down_factors,
    tenant_up_factors,
    cotangent,
    block_tenant_index,
    ranks,
):
    num_peers = lax.axis_size("dp")
    my_index = lax.axis_index("dp")
    row_count, feat_width = tokens.shape
    block_count = row_count // BLOCK
    held_tenant_count = tenant_down_factors.shape[0]
    rank_padding = tenant_down_factors.shape[2]
    count_of_tenants = held_tenant_count * num_peers
    piece_width = feat_width // num_peers
    block_total = block_count * num_peers
    rank_positions = jnp.arange(rank_padding, dtype=jnp.int32)
    kept_ranks = (rank_positions[None, :] < ranks[:, None]).astype(jnp.float32)
    coef_table = kept_ranks * (16.0 / ranks.astype(jnp.float32))[:, None]
    tenant_range = jnp.arange(count_of_tenants, dtype=jnp.int32)
    my_tenants = lax.dynamic_slice_in_dim(block_tenant_index, my_index * block_count, block_count)
    select_onehot = (my_tenants[:, None] == tenant_range[None, :]).astype(jnp.float32)
    block_coef = jnp.dot(select_onehot, coef_table, precision=lax.Precision.HIGHEST)
    stacked_factors = jnp.concatenate([tenant_down_factors, tenant_up_factors], axis=2)
    split_factors = stacked_factors.reshape(
        held_tenant_count, num_peers, piece_width, 2 * rank_padding
    )
    received = lax.all_to_all(split_factors, "dp", split_axis=1, concat_axis=0, tiled=True)
    piece_table = received.reshape(count_of_tenants, piece_width * 2 * rank_padding)
    selection = block_tenant_index.reshape(num_peers, block_count)
    outgoing = piece_table[selection].reshape(num_peers, block_count, piece_width, 2 * rank_padding)
    arrived = lax.all_to_all(outgoing, "dp", split_axis=0, concat_axis=2, tiled=True)
    factors = arrived.reshape(block_count, feat_width, 2 * rank_padding)
    down_factor = factors[:, :, :rank_padding]
    up_factor = factors[:, :, rank_padding:]
    tok_blocks = tokens.reshape(block_count, BLOCK, feat_width)
    low_partial = jnp.einsum(
        "bid,bdr->bir", tok_blocks, down_factor, preferred_element_type=jnp.float32
    )
    pre_low = lax.psum(low_partial.astype(jnp.bfloat16), "mp").astype(jnp.float32)
    low_rank = (pre_low * block_coef[:, None, :]).astype(jnp.bfloat16)
    weights_all = lax.all_gather(frozen_base_weight, "dp", axis=1, tiled=True)
    base_terms = jnp.dot(tokens, weights_all, preferred_element_type=jnp.float32)
    base_share = lax.psum_scatter(
        base_terms.astype(jnp.bfloat16), "mp", scatter_dimension=1, tiled=True
    ).astype(jnp.float32)
    adapter_out = jnp.einsum(
        "bir,ber->bie", low_rank, up_factor, preferred_element_type=jnp.float32
    )
    layer_out = (base_share + adapter_out.reshape(row_count, feat_width)).astype(jnp.bfloat16)
    cot_blocks = cotangent.reshape(block_count, BLOCK, feat_width)
    dlow_partial = jnp.einsum(
        "bie,ber->bir", cot_blocks, up_factor, preferred_element_type=jnp.float32
    )
    pre_dlow = lax.psum(dlow_partial.astype(jnp.bfloat16), "mp").astype(jnp.float32)
    dlow_rank = (pre_dlow * block_coef[:, None, :]).astype(jnp.bfloat16)
    full_cotangent = lax.all_gather(cotangent, "mp", axis=1, tiled=True)
    base_grad = lax.dot_general(
        full_cotangent, weights_all, (((1,), (1,)), ((), ())), preferred_element_type=jnp.float32
    )
    adapter_grad = jnp.einsum(
        "bir,bdr->bid", dlow_rank, down_factor, preferred_element_type=jnp.float32
    )
    input_grad = (base_grad + adapter_grad.reshape(row_count, feat_width)).astype(jnp.bfloat16)
    block_down = jnp.einsum(
        "bid,bir->bdr", tok_blocks, dlow_rank, preferred_element_type=jnp.float32
    )
    block_up = jnp.einsum("bie,bir->ber", cot_blocks, low_rank, preferred_element_type=jnp.float32)
    block_grads = jnp.concatenate([block_down, block_up], axis=2)
    split_grads = block_grads.reshape(block_count, num_peers, piece_width, 2 * rank_padding)
    grad_arrived = lax.all_to_all(
        split_grads.astype(jnp.bfloat16), "dp", split_axis=1, concat_axis=0, tiled=True
    ).astype(split_grads.dtype)
    grad_rows = grad_arrived.reshape(block_total, piece_width * 2 * rank_padding)
    tenant_onehot = (block_tenant_index[None, :] == tenant_range[:, None]).astype(jnp.float32)
    tenant_sums = jnp.dot(tenant_onehot, grad_rows, precision=lax.Precision.HIGHEST)
    owner_bound = tenant_sums.reshape(num_peers, held_tenant_count, piece_width, 2 * rank_padding)
    owned_grads = lax.all_to_all(
        owner_bound.astype(jnp.bfloat16), "dp", split_axis=0, concat_axis=2, tiled=True
    ).astype(owner_bound.dtype)
    owned_grads = owned_grads.reshape(held_tenant_count, feat_width, 2 * rank_padding)
    down_grad = owned_grads[:, :, :rank_padding]
    up_grad = owned_grads[:, :, rank_padding:]
    return (layer_out, input_grad, down_grad, up_grad)


def solution(mesh):
    return jax.shard_map(
        local,
        mesh=mesh,
        in_specs=(
            P("dp", "mp"),
            P("mp", "dp"),
            P("dp", "mp", None),
            P("dp", "mp", None),
            P("dp", "mp"),
            P(),
            P(),
        ),
        out_specs=(P("dp", "mp"), P("dp", "mp"), P("dp", "mp", None), P("dp", "mp", None)),
        check_vma=False,
    )
```

profile of v0, /device:TPU:8, one launch (start us, length us, event | category | flops | bytes accessed | tf_op | source)
XLA Modules:
  0.0 286.6 jit_solution(3312873384921859337)
XLA Ops:
  8.1 0.7 all-gather.3.cloned.1.call-update
  8.7 1.2 copy.26
  10.0 1.2 copy.25
  11.5 0.9 copy.27
  12.4 11.3 %all-to-all-start = ((bf16[2,32,32,128]{3,2,0,1:T(8,128)(2,1)}), bf16[2,32,32,128]{3,2,0,1:T(8,128)(2,1)S(1)}, u32[]{:S(2)}, u32[]{:S(2)}) async-start(bf16[2,32,32,128]{3,2,0,1:T(8,128)(2,1)} %copy.27), calls=%async_computation.1 | async-start | bytes 1048576 | tf_op jit(solution)/shard_map/all_to_all | solution.py:38
  23.7 0.8 reshape.107
  24.6 20.3 %all-to-all-done = bf16[2,32,32,128]{3,2,0,1:T(8,128)(2,1)S(1)} async-done(((bf16[2,32,32,128]{3,2,0,1:T(8,128)(2,1)}), bf16[2,32,32,128]{3,2,0,1:T(8,128)(2,1)S(1)}, u32[]{:S(2)}, u32[]{:S(2)}) %all-to-all-start) | async-done | bytes 524320 | tf_op jit(solution)/shard_map/all_to_all | solution.py:38
  45.1 1.0 gather_fusion
  46.3 30.9 %all_to_all.54 = bf16[32,3,32,128]{3,2,1,0:T(8,128)(2,1)S(1)} all-to-all(bf16[32,3,32,128]{3,2,1,0:T(8,128)(2,1)S(1)} %bitcast.90), channel_id=1, replica_groups=mesh['dp'=32,'mp'=8] {'dp'}, dimensions={0} | all-to-all | bytes 1572864 | tf_op jit(solution)/shard_map/all_to_all | solution.py:42
  77.3 1.1 fusion.4
  78.3 1.4 fusion.5
  79.9 0.7 all-gather.5.cloned.1.call-update
  80.6 103.5 %all-gather.3.cloned.1.call-done = bf16[1024,8192]{1,0:T(8,128)(2,1)} async-done(((bf16[1024,256]{1,0:T(8,128)(2,1)}), bf16[1024,8192]{1,0:T(8,128)(2,1)}) %all-gather.3.cloned.1.call-update) | async-done | bytes 16777232 | tf_op jit(solution)/shard_map/all_gather | solution.py:52
  184.1 14.3 %convolution_convert_fusion = bf16[384,8192]{1,0:T(8,128)(2,1)} fusion(bf16[384,1024]{1,0:T(8,128)(2,1)S(1)} %copy-done, bf16[1024,8192]{1,0:T(8,128)(2,1)} %all-gather.3.cloned.1.call-done), kind=kOutput, calls=%fused_computation.1 | convolution fusion | flops 6445596672 | bytes 23855104 | tf_op jit(solution)/shard_map/dot_general | solution.py:53
  198.5 0.6 copy-done.5
  199.6 1.1 fusion.3
  200.7 1.1 fusion.2
  202.3 0.9 copy.32
  203.2 5.5 %all-to-all-start.2 = ((bf16[3,32,32,128]{3,2,0,1:T(8,128)(2,1)}), bf16[3,32,32,128]{3,2,0,1:T(8,128)(2,1)S(1)}, u32[]{:S(2)}, u32[]{:S(2)}) async-start(bf16[3,32,32,128]{3,2,0,1:T(8,128)(2,1)} %copy.32), calls=%async_computation.3 | async-start | bytes 1572864 | tf_op jit(solution)/shard_map/all_to_all | solution.py:81
  208.8 20.0 %all-to-all-done.2 = bf16[3,32,32,128]{3,2,0,1:T(8,128)(2,1)S(1)} async-done(((bf16[3,32,32,128]{3,2,0,1:T(8,128)(2,1)}), bf16[3,32,32,128]{3,2,0,1:T(8,128)(2,1)S(1)}, u32[]{:S(2)}, u32[]{:S(2)}) %all-to-all-start.2) | async-done | bytes 786464 | tf_op jit(solution)/shard_map/all_to_all | solution.py:81
  228.8 0.4 convolution_convert_fusion.1
  229.2 1.0 copy.34
  230.2 5.3 %all-to-all-start.3 = ((bf16[32,2,32,128]{3,2,1,0:T(8,128)(2,1)}), bf16[32,2,32,128]{3,2,1,0:T(8,128)(2,1)}, u32[]{:S(2)}, u32[]{:S(2)}) async-start(bf16[32,2,32,128]{3,2,1,0:T(8,128)(2,1)} %copy.34), calls=%async_computation.4 | async-start | bytes 1048576 | tf_op jit(solution)/shard_map/all_to_all | solution.py:88
  235.5 0.7 fusion.7
  236.2 1.7 fusion.11
  237.9 12.4 %all-to-all-done.3 = bf16[32,2,32,128]{3,2,1,0:T(8,128)(2,1)} async-done(((bf16[32,2,32,128]{3,2,1,0:T(8,128)(2,1)}), bf16[32,2,32,128]{3,2,1,0:T(8,128)(2,1)}, u32[]{:S(2)}, u32[]{:S(2)}) %all-to-all-start.3) | async-done | bytes 524320 | tf_op jit(solution)/shard_map/all_to_all | solution.py:88
  250.3 1.2 bitcast_convert_fusion
  251.5 1.6 fusion.24
  253.1 2.3 copy.36
  255.5 2.3 copy.37
  257.8 19.0 %fusion = bf16[384,1024]{1,0:T(8,128)(2,1)} fusion(f32[3,128,1024]{2,1,0:T(8,128)} %fusion.11, bf16[384,8192]{1,0:T(8,128)(2,1)} %all-gather.5.cloned.1.call-done, bf16[1024,8192]{1,0:T(8,128)(2,1)} %all-gather.3.cloned.1.call-done), kind=kOutput, calls=%fused_computation.3 | convolution fusion | flops 6443237376 | bytes 25427968 | tf_op jit(solution)/shard_map/dot_general | solution.py:68
  276.8 2.4 fusion.1
  (35 shorter events, 2.0 us)
Async XLA Ops:
  8.0 69.3 %copy-start = (bf16[384,1024]{1,0:T(8,128)(2,1)S(1)}, bf16[384,1024]{1,0:T(8,128)(2,1)}, u32[]{:S(2)}) copy-start(bf16[384,1024]{1,0:T(8,128)(2,1)} %param.7) | copy-start | bytes 2359300
  8.0 176.1 %all-gather.3.cloned.1.call-start = ((), (), s32[]{:S(2)}) async-start(), calls=%async_computation.5 | async-start | bytes 17301504 | tf_op jit(solution)/shard_map/all_gather | solution.py:52
  12.4 32.5 %all-to-all-start = ((bf16[2,32,32,128]{3,2,0,1:T(8,128)(2,1)}), bf16[2,32,32,128]{3,2,0,1:T(8,128)(2,1)S(1)}, u32[]{:S(2)}, u32[]{:S(2)}) async-start(bf16[2,32,32,128]{3,2,0,1:T(8,128)(2,1)} %copy.27), calls=%async_computation.1 | async-start | bytes 1048576 | tf_op jit(solution)/shard_map/all_to_all | solution.py:38
  23.7 175.7 %all-reduce.3.cloned.1.call-start = ((), (), s32[]{:S(2)}) async-start(), calls=%async_computation.8 | async-start | bytes 196608 | tf_op jit(solution)/shard_map/psum | solution.py:50
  45.1 33.2 %copy-start.1 = (bf16[384,1024]{1,0:T(8,128)(2,1)S(1)}, bf16[384,1024]{1,0:T(8,128)(2,1)}, u32[]{:S(2)}) copy-start(bf16[384,1024]{1,0:T(8,128)(2,1)} %param.11) | copy-start | bytes 2359300
  79.8 178.0 %all-gather.5.cloned.1.call-start = ((), (), s32[]{:S(2)}) async-start(), calls=%async_computation.7 | async-start | bytes 7077888 | tf_op jit(solution)/shard_map/all_gather | solution.py:67
  80.6 196.3 %reduce-scatter.2.cloned.1.call-start = ((), (), s32[]{:S(2)}) async-start(), calls=%async_computation.6 | async-start | bytes 7077888 | tf_op jit(solution)/shard_map/reduce_scatter | solution.py:54
  198.4 0.7 copy-start.5
  198.4 0.7 copy-start.6
  198.4 1.2 copy-start.2
  199.4 36.1 %copy-start.4 = (bf16[3,128,64]{1,2,0:T(8,128)(2,1)S(1)}, bf16[3,128,64]{1,2,0:T(8,128)(2,1)}, u32[]{:S(2)}) copy-start(bf16[3,128,64]{1,2,0:T(8,128)(2,1)} %get-tuple-element.12) | copy-start | bytes 147460
  201.8 34.4 %copy-start.3 = (bf16[3,128,64]{1,2,0:T(8,128)(2,1)S(1)}, bf16[3,128,64]{1,2,0:T(8,128)(2,1)}, u32[]{:S(2)}) copy-start(bf16[3,128,64]{1,2,0:T(8,128)(2,1)} %get-tuple-element.13) | copy-start | bytes 147460
  203.2 25.6 %all-to-all-start.2 = ((bf16[3,32,32,128]{3,2,0,1:T(8,128)(2,1)}), bf16[3,32,32,128]{3,2,0,1:T(8,128)(2,1)S(1)}, u32[]{:S(2)}, u32[]{:S(2)}) async-start(bf16[3,32,32,128]{3,2,0,1:T(8,128)(2,1)} %copy.32), calls=%async_computation.3 | async-start | bytes 1572864 | tf_op jit(solution)/shard_map/all_to_all | solution.py:81
  230.2 20.2 %all-to-all-start.3 = ((bf16[32,2,32,128]{3,2,1,0:T(8,128)(2,1)}), bf16[32,2,32,128]{3,2,1,0:T(8,128)(2,1)}, u32[]{:S(2)}, u32[]{:S(2)}) async-start(bf16[32,2,32,128]{3,2,1,0:T(8,128)(2,1)} %copy.34), calls=%async_computation.4 | async-start | bytes 1048576 | tf_op jit(solution)/shard_map/all_to_all | solution.py:88
Sparse Core Ops, SparseCore 0:
  11.6 172.4 all-gather.2
  186.1 47.7 all-gather.4
Sparse Core Ops, SparseCore 1:
  79.9 59.3 all-reduce.2
  198.5 54.7 reduce-scatter.1
where the time goes:
time: 287 us
  waiting for transfers between devices  158 us (55%)
  matrix products  41.1 us (14%)
  blocking collectives  30.9 us (11%)
  starting transfers between devices  22.3 us (8%)
  between operations  15.7 us (5%)
  local copies, waits for them, and re-layouts  15.2 us (5%)
  other arithmetic  3.91 us (1%)
    all_gather x1, waiting for transfers between devices, local(): weights_all = lax.all_gather(frozen_base_weight, 'dp', axis=1, tiled=True)  103 us
    all_to_all x1, blocking collectives, local(): lax.all_to_all(outgoing, 'dp', split_axis=0, concat_axis=2, tiled=True)  30.9 us
    all_to_all x1, waiting for transfers between devices, local(): lax.all_to_all(split_factors, 'dp', split_axis=1, concat_axis=0, tiled=True)  20.3 us
    all_to_all x1, waiting for transfers between devices, local(): lax.all_to_all(split_grads.astype(jnp.bfloat16), 'dp', split_axis=1, conc...  20 us
    dot_general x1, matrix products, local(): lax.dot_general(full_cotangent, weights_all, (((1,), (1,)), ((), ())), pr...  19 us
    dot_general x1, matrix products, local(): jnp.dot(tokens, weights_all, preferred_element_type=jnp.float32)  14.3 us
    all_to_all x1, waiting for transfers between devices, local(): lax.all_to_all(owner_bound.astype(jnp.bfloat16), 'dp', split_axis=0, conc...  12.4 us
    all_to_all x1, starting transfers between devices, local(): lax.all_to_all(split_factors, 'dp', split_axis=1, concat_axis=0, tiled=True)  11.3 us
  transfers between devices with their start and end apart: 7, of which 4 were waited for; matrix products, arithmetic and copies ran while one was open for 20% of the time, Pallas kernels for 0%

commit v1 on v0

--- a/solution.py
+++ b/solution.py
@@ -85,8 +85,14 @@
     tenant_onehot = (block_tenant_index[None, :] == tenant_range[:, None]).astype(jnp.float32)
     tenant_sums = jnp.dot(tenant_onehot, grad_rows, precision=lax.Precision.HIGHEST)
     owner_bound = tenant_sums.reshape(num_peers, held_tenant_count, piece_width, 2 * rank_padding)
-    owned_grads = lax.all_to_all(
-        owner_bound.astype(jnp.bfloat16), "dp", split_axis=0, concat_axis=2, tiled=True
+    owned_grads = jnp.concatenate(
+        lax.all_to_all(
+            jnp.stack(jnp.split(owner_bound.astype(jnp.bfloat16), lax.axis_size("dp"), axis=0)),
+            "dp",
+            0,
+            0,
+        ),
+        axis=2,
     ).astype(owner_bound.dtype)
     owned_grads = owned_grads.reshape(held_tenant_count, feat_width, 2 * rank_padding)
     down_grad = owned_grads[:, :, :rank_padding]

time: 287 us -> 336 us (1.17)
  waiting for transfers between devices: 158 us -> 181 us
  local copies, waits for them, and re-layouts: 15.2 us -> 36.5 us
  starting transfers between devices: 22.3 us -> 28.3 us
  blocking collectives: 30.9 us -> 26.3 us
    psum x1, waiting for transfers between devices: 0.01 us -> 56.7 us  [local(): lax.psum(low_partial.astype(jnp.bfloat16), 'mp').astype(jnp.float32)]
    all_gather x1, waiting for transfers between devices: 103 us -> 63.4 us  [local(): weights_all = lax.all_gather(frozen_base_weight, 'dp', axis=1, tiled=True)]
    unnamed x20 -> x51, local copies, waits for them, and re-layouts: 8.36 us -> 27.7 us
    all_to_all x1, waiting for transfers between devices: 20 us -> 30.5 us  [local(): lax.all_to_all(split_grads.astype(jnp.bfloat16), 'dp', split_axis=1, conc...]
    all_to_all x1, blocking collectives: 30.9 us -> 26.3 us  [local(): lax.all_to_all(outgoing, 'dp', split_axis=0, concat_axis=2, tiled=True)]
    all_to_all x1, starting transfers between devices: 5.54 us -> 9.54 us  [local(): lax.all_to_all(split_grads.astype(jnp.bfloat16), 'dp', split_axis=1, conc...]
    all_to_all x1, waiting for transfers between devices: 20.3 us -> 16.8 us  [local(): lax.all_to_all(split_factors, 'dp', split_axis=1, concat_axis=0, tiled=True)]
  transfers between devices with their start and end apart: 7 -> 7, of which waited for: 4 -> 5; matrix products, arithmetic and copies ran while one was open for 20% -> 21% of each run, Pallas kernels for 0% -> 0%
where the time goes in v1:
time: 336 us; the launch traced here: 334 us
  waiting for transfers between devices  181 us (54%)
  matrix products  41.4 us (12%)
  local copies, waits for them, and re-layouts  36.5 us (11%)
  starting transfers between devices  28.3 us (8%)
  blocking collectives  26.3 us (8%)
  between operations  15.8 us (5%)
  other arithmetic  3.91 us (1%)
    all_gather x1, waiting for transfers between devices, local(): weights_all = lax.all_gather(frozen_base_weight, 'dp', axis=1, tiled=True)  63.4 us
    psum x1, waiting for transfers between devices, local(): lax.psum(low_partial.astype(jnp.bfloat16), 'mp').astype(jnp.float32)  56.7 us
    all_to_all x1, waiting for transfers between devices, local(): lax.all_to_all(split_grads.astype(jnp.bfloat16), 'dp', split_axis=1, conc...  30.5 us
    unnamed x51, local copies, waits for them, and re-layouts  27.7 us
    all_to_all x1, blocking collectives, local(): lax.all_to_all(outgoing, 'dp', split_axis=0, concat_axis=2, tiled=True)  26.3 us
    dot_general x1, matrix products, local(): lax.dot_general(full_cotangent, weights_all, (((1,), (1,)), ((), ())), pr...  19.4 us
    all_to_all x1, waiting for transfers between devices, local(): lax.all_to_all(split_factors, 'dp', split_axis=1, concat_axis=0, tiled=True)  16.8 us
    dot_general x1, matrix products, local(): jnp.dot(tokens, weights_all, preferred_element_type=jnp.float32)  14.3 us
  transfers between devices with their start and end apart: 7, of which 5 were waited for; matrix products, arithmetic and copies ran while one was open for 21% of the time, Pallas kernels for 0%

profile of v1, /device:TPU:8, one launch (start us, length us, event | category | flops | bytes accessed | tf_op | source)
XLA Modules:
  0.0 333.7 jit_solution(14265051133832841151)
XLA Ops:
  8.0 1.3 copy.882
  9.3 1.2 copy.881
  10.8 0.9 copy.883
  11.7 11.3 %all-to-all-start = ((bf16[2,32,32,128]{3,2,0,1:T(8,128)(2,1)}), bf16[2,32,32,128]{3,2,0,1:T(8,128)(2,1)S(1)}, u32[]{:S(2)}, u32[]{:S(2)}) async-start(bf16[2,32,32,128]{3,2,0,1:T(8,128)(2,1)} %copy.883), calls=%async_computation.1 | async-start | bytes 1048576 | tf_op jit(solution)/shard_map/all_to_all | solution.py:38
  23.1 0.8 reshape.107
  24.0 16.8 %all-to-all-done = bf16[2,32,32,128]{3,2,0,1:T(8,128)(2,1)S(1)} async-done(((bf16[2,32,32,128]{3,2,0,1:T(8,128)(2,1)}), bf16[2,32,32,128]{3,2,0,1:T(8,128)(2,1)S(1)}, u32[]{:S(2)}, u32[]{:S(2)}) %all-to-all-start) | async-done | bytes 524320 | tf_op jit(solution)/shard_map/all_to_all | solution.py:38
  41.1 1.9 gather_fusion
  43.0 1.4 copy.934
  44.4 26.3 %all_to_all.50 = bf16[32,3,32,128]{3,2,1,0:T(8,128)(2,1)S(1)} all-to-all(bf16[32,3,32,128]{3,2,1,0:T(8,128)(2,1)S(1)} %bitcast.155), channel_id=1, replica_groups=mesh['dp'=32,'mp'=8] {'dp'}, dimensions={0} | all-to-all | bytes 1572864 | tf_op jit(solution)/shard_map/all_to_all | solution.py:42
  70.7 1.1 fusion.4
  71.8 1.4 fusion.5
  74.8 56.7 %all-reduce.3.cloned.1.call-done = (bf16[3,128,64]{1,2,0:T(8,128)(2,1)}, bf16[3,128,64]{1,2,0:T(8,128)(2,1)}) async-done(((bf16[3,128,64]{1,2,0:T(8,128)(2,1)}, bf16[3,128,64]{1,2,0:T(8,128)(2,1)}), (bf16[3,128,64]{1,2,0:T(8,128)(2,1)}, bf16[3,128,64]{1,2,0:T(8,128)(2,1)})) %all-reduce.3.cloned.1.call-update) | async-done | bytes 98320 | tf_op jit(solution)/shard_map/psum | solution.py:50
  131.5 1.1 fusion.3
  132.6 1.1 fusion.2
  134.2 0.9 copy.890
  135.1 9.5 %all-to-all-start.2 = ((bf16[3,32,32,128]{3,2,0,1:T(8,128)(2,1)}), bf16[3,32,32,128]{3,2,0,1:T(8,128)(2,1)S(1)}, u32[]{:S(2)}, u32[]{:S(2)}) async-start(bf16[3,32,32,128]{3,2,0,1:T(8,128)(2,1)} %copy.890), calls=%async_computation.3 | async-start | bytes 1572864 | tf_op jit(solution)/shard_map/all_to_all | solution.py:81
  144.7 30.5 %all-to-all-done.2 = bf16[3,32,32,128]{3,2,0,1:T(8,128)(2,1)S(1)} async-done(((bf16[3,32,32,128]{3,2,0,1:T(8,128)(2,1)}), bf16[3,32,32,128]{3,2,0,1:T(8,128)(2,1)S(1)}, u32[]{:S(2)}, u32[]{:S(2)}) %all-to-all-start.2) | async-done | bytes 786464 | tf_op jit(solution)/shard_map/all_to_all | solution.py:81
  175.3 63.4 %all-gather.3.cloned.1.call-done = bf16[1024,8192]{1,0:T(8,128)(2,1)} async-done(((bf16[1024,256]{1,0:T(8,128)(2,1)}), bf16[1024,8192]{1,0:T(8,128)(2,1)}) %all-gather.3.cloned.1.call-update) | async-done | bytes 16777232 | tf_op jit(solution)/shard_map/all_gather | solution.py:52
  238.7 14.3 %convolution_convert_fusion = bf16[384,8192]{1,0:T(8,128)(2,1)} fusion(bf16[384,1024]{1,0:T(8,128)(2,1)S(1)} %copy-done, bf16[1024,8192]{1,0:T(8,128)(2,1)} %all-gather.3.cloned.1.call-done), kind=kOutput, calls=%fused_computation.1 | convolution fusion | flops 6445596672 | bytes 23855104 | tf_op jit(solution)/shard_map/dot_general | solution.py:53
  253.9 0.6 constant_dynamic-update-slice_fusion.31
  261.8 0.7 fusion.25
  262.6 0.6 constant_dynamic-update-slice_fusion.18
  274.1 7.3 %all-to-all-start.3 = ((bf16[32,1,2,32,128]{4,3,2,1,0:T(8,128)(2,1)}), bf16[32,1,2,32,128]{4,3,2,1,0:T(8,128)(2,1)}, u32[]{:S(2)}, u32[]{:S(2)}) async-start(bf16[32,1,2,32,128]{4,3,2,1,0:T(8,128)(2,1)} %constant_dynamic-update-slice_fusion), calls=%async_computation.4 | async-start | bytes 1048576 | tf_op jit(solution)/shard_map/all_to_all | solution.py:89
  281.4 0.7 fusion.7
  282.2 1.7 fusion.11
  283.9 13.0 %all-to-all-done.3 = bf16[32,1,2,32,128]{4,3,2,1,0:T(8,128)(2,1)} async-done(((bf16[32,1,2,32,128]{4,3,2,1,0:T(8,128)(2,1)}), bf16[32,1,2,32,128]{4,3,2,1,0:T(8,128)(2,1)}, u32[]{:S(2)}, u32[]{:S(2)}) %all-to-all-start.3) | async-done | bytes 524320 | tf_op jit(solution)/shard_map/all_to_all | solution.py:89
  296.9 1.2 convert_bitcast_fusion
  298.2 1.6 fusion.24
  299.8 2.4 copy.895
  302.1 2.4 copy.896
  304.5 19.4 %fusion = bf16[384,1024]{1,0:T(8,128)(2,1)} fusion(f32[3,128,1024]{2,1,0:T(8,128)} %fusion.11, bf16[384,8192]{1,0:T(8,128)(2,1)} %all-gather.5.cloned.1.call-done, bf16[1024,8192]{1,0:T(8,128)(2,1)} %all-gather.3.cloned.1.call-done), kind=kOutput, calls=%fused_computation.3 | convolution fusion | flops 6443237376 | bytes 25427968 | tf_op jit(solution)/shard_map/dot_general | solution.py:68
  323.9 2.4 fusion.1
  (73 shorter events, 22.1 us)
Async XLA Ops:
  8.0 62.7 %copy-start = (bf16[384,1024]{1,0:T(8,128)(2,1)S(1)}, bf16[384,1024]{1,0:T(8,128)(2,1)}, u32[]{:S(2)}) copy-start(bf16[384,1024]{1,0:T(8,128)(2,1)} %param.7) | copy-start | bytes 2359300
  11.7 29.0 %all-to-all-start = ((bf16[2,32,32,128]{3,2,0,1:T(8,128)(2,1)}), bf16[2,32,32,128]{3,2,0,1:T(8,128)(2,1)S(1)}, u32[]{:S(2)}, u32[]{:S(2)}) async-start(bf16[2,32,32,128]{3,2,0,1:T(8,128)(2,1)} %copy.883), calls=%async_computation.1 | async-start | bytes 1048576 | tf_op jit(solution)/shard_map/all_to_all | solution.py:38
  23.0 108.4 %all-reduce.3.cloned.1.call-start = ((), (), s32[]{:S(2)}) async-start(), calls=%async_computation.8 | async-start | bytes 196608 | tf_op jit(solution)/shard_map/psum | solution.py:50
  41.1 30.8 %copy-start.1 = (bf16[384,1024]{1,0:T(8,128)(2,1)S(1)}, bf16[384,1024]{1,0:T(8,128)(2,1)}, u32[]{:S(2)}) copy-start(bf16[384,1024]{1,0:T(8,128)(2,1)} %param.11) | copy-start | bytes 2359300
  43.0 31.5 %copy-start.5 = (s32[96]{0:T(128)S(1)}, s32[96]{0:T(128)}, u32[]{:S(2)}) copy-start(s32[96]{0:T(128)} %param.12) | copy-start | bytes 1156
  43.0 31.6 %copy-start.6 = (s32[64]{0:T(128)S(1)}, s32[64]{0:T(128)}, u32[]{:S(2)}) copy-start(s32[64]{0:T(128)} %param.13) | copy-start | bytes 772
  43.0 88.5 %copy-start.2 = (bf16[384,1024]{1,0:T(8,128)(2,1)S(1)}, bf16[384,1024]{1,0:T(8,128)(2,1)}, u32[]{:S(2)}) copy-start(bf16[384,1024]{1,0:T(8,128)(2,1)} %param.11) | copy-start | bytes 2359300
  73.3 165.4 %all-gather.3.cloned.1.call-start = ((), (), s32[]{:S(2)}) async-start(), calls=%async_computation.5 | async-start | bytes 17301504 | tf_op jit(solution)/shard_map/all_gather | solution.py:52
  73.9 230.6 %all-gather.5.cloned.1.call-start = ((), (), s32[]{:S(2)}) async-start(), calls=%async_computation.7 | async-start | bytes 7077888 | tf_op jit(solution)/shard_map/all_gather | solution.py:67
  135.1 40.1 %all-to-all-start.2 = ((bf16[3,32,32,128]{3,2,0,1:T(8,128)(2,1)}), bf16[3,32,32,128]{3,2,0,1:T(8,128)(2,1)S(1)}, u32[]{:S(2)}, u32[]{:S(2)}) async-start(bf16[3,32,32,128]{3,2,0,1:T(8,128)(2,1)} %copy.890), calls=%async_computation.3 | async-start | bytes 1572864 | tf_op jit(solution)/shard_map/all_to_all | solution.py:81
  144.6 179.3 %reduce-scatter.2.cloned.1.call-start = ((), (), s32[]{:S(2)}) async-start(), calls=%async_computation.6 | async-start | bytes 7077888 | tf_op jit(solution)/shard_map/reduce_scatter | solution.py:54
  253.0 28.4 %copy-start.4 = (bf16[3,128,64]{1,2,0:T(8,128)(2,1)S(1)}, bf16[3,128,64]{1,2,0:T(8,128)(2,1)}, u32[]{:S(2)}) copy-start(bf16[3,128,64]{1,2,0:T(8,128)(2,1)} %get-tuple-element.132) | copy-start | bytes 147460
  253.0 29.1 %copy-start.3 = (bf16[3,128,64]{1,2,0:T(8,128)(2,1)S(1)}, bf16[3,128,64]{1,2,0:T(8,128)(2,1)}, u32[]{:S(2)}) copy-start(bf16[3,128,64]{1,2,0:T(8,128)(2,1)} %get-tuple-element.133) | copy-start | bytes 147460
  274.1 22.8 %all-to-all-start.3 = ((bf16[32,1,2,32,128]{4,3,2,1,0:T(8,128)(2,1)}), bf16[32,1,2,32,128]{4,3,2,1,0:T(8,128)(2,1)}, u32[]{:S(2)}, u32[]{:S(2)}) async-start(bf16[32,1,2,32,128]{4,3,2,1,0:T(8,128)(2,1)} %constant_dynamic-update-slice_fusion), calls=%async_computation.4 | async-start | bytes 1048576 | tf_op jit(solution)/shard_map/all_to_all | solution.py:89
Sparse Core Ops, SparseCore 0:
  73.4 58.0 all-reduce.2
  253.2 57.4 reduce-scatter.1
Sparse Core Ops, SparseCore 1:
  76.5 162.1 all-gather.2
  240.6 50.6 all-gather.4
